TPU v7x, 32 devices: a whole 2x2x4 slice. The times are simulated.
32 devices in a mesh: stream: 2 (over y), dp: 16 (over z, x, core).
Axes of the slice: x: 2, y: 2, z: 4, core: 2. Of those that a mesh axis runs over, the one named last changes fastest.
Arguments:
- states: bfloat16 [2, 32, 96, 1024], P('stream', 'dp'), may hold values from -6 to 6
- out_grad: bfloat16 [2, 32, 96, 1024], P('stream', 'dp'), may hold values from -6 to 6
- co_params: float32 [2, 8398848], P('stream', 'dp')
- self_params: float32 [2, 7088128], P('stream', 'dp')
- text_lengths: int32 [32], P('dp'), may hold values from 1 to 128, as said below
- region_counts: int32 [32], P('dp'), may hold values from 1 to 96, as said below
Outputs:
- out_states: bfloat16 [2, 32, 96, 1024], P('stream', 'dp')
- states_grad: float32 [2, 32, 96, 1024], P('stream', 'dp')
- co_grad: float32 [2, 8398848], P('stream', 'dp')
- self_grad: float32 [2, 7088128], P('stream', 'dp')
Inputs may be any that keep to these rules, and one draw needn't show every extreme that they name: `text_lengths`: some sequence has exactly 128 text tokens. `region_counts`: some image has exactly 96 regions.
All inputs are finite; a program needn't handle non-finite values.
Results may differ from a plain program's by a relative error of at most 0.02.
Values may be sent and summed in bfloat16 or wider, within the bound.
A program may use at most 320 MiB of HBM per device.

v0:
```python
import functools
import math

import jax
import jax.numpy as jnp
from jax import lax
from jax.sharding import PartitionSpec as P

DT = 768
HT = 12
FT = 3072
DI = 1024
HI = 8
FI = 1024
DC = 1024
HC = 8
LT = 128
LI = 96


norm_eps = 1e-12
masked_score = -1000000000.0


def from_partner(x, axis, apart):
    return lax.ppermute(x, axis, [(i, i ^ 1 << apart) for i in range(lax.axis_size(axis))])


def shapes(model_width, other_width, inner_width, hidden):
    return [
        (model_width, inner_width),
        (inner_width,),
        (other_width, inner_width),
        (other_width, inner_width),
        (inner_width,),
        (inner_width, model_width),
        (model_width,),
        (model_width,),
        (model_width,),
        (model_width, hidden),
        (hidden,),
        (hidden, model_width),
        (model_width,),
        (model_width,),
        (model_width,),
    ]


def unpack(flat_values, layout):
    pieces = []
    offset = 0
    for piece_shape in layout:
        piece_count = math.prod(piece_shape)
        pieces.append(flat_values[offset : offset + piece_count].reshape(piece_shape))
        offset += piece_count
    return pieces


def pack(pieces, total_size):
    flat_values = jnp.concatenate([piece.reshape(-1) for piece in pieces])
    return jnp.pad(flat_values, (0, total_size - flat_values.shape[0]))


def as_rows(flat_values):
    return flat_values.reshape(flat_values.shape[0] // 128, 128)


def layer_norm(row_values, norm_gain, norm_shift):
    centre = row_values - jnp.mean(row_values, axis=-1, keepdims=True)
    spread = jnp.mean(centre * centre, axis=-1, keepdims=True)
    return centre * lax.rsqrt(spread + norm_eps) * norm_gain + norm_shift


def gelu_exact(values):
    return jax.nn.gelu(values, approximate=False)


def product(left_side, right_side):
    return jnp.dot(left_side, right_side, preferred_element_type=jnp.float32)


def product_tn(left_side, right_side):
    return lax.dot_general(
        left_side, right_side, (((0,), (0,)), ((), ())), preferred_element_type=jnp.float32
    )


def product_nt(left_side, right_side):
    return lax.dot_general(
        left_side, right_side, (((1,), (1,)), ((), ())), preferred_element_type=jnp.float32
    )


def column_sums(values_low):
    return jnp.sum(values_low.astype(jnp.float32), axis=0)


def scores_of(queries, key_rows, key_valid, head_count):
    seq_count, length, inner_width = queries.shape
    head_size = inner_width // head_count
    query_heads = queries.reshape(seq_count, length, head_count, head_size)
    key_heads = key_rows.reshape(seq_count, key_rows.shape[1], head_count, head_size)
    scores = jnp.einsum(
        "sqhd,skhd->shqk", query_heads, key_heads, preferred_element_type=jnp.float32
    )
    scores = scores * (1.0 / math.sqrt(head_size))
    return jnp.where(key_valid[:, None, None, :], scores, masked_score)


def attn_forward(queries, key_rows, value_rows, key_valid, head_count):
    seq_count, length, inner_width = queries.shape
    head_size = inner_width // head_count
    scores = scores_of(queries, key_rows, key_valid, head_count)
    largest = jnp.max(scores, axis=-1, keepdims=True)
    log_total = largest + jnp.log(jnp.sum(jnp.exp(scores - largest), axis=-1, keepdims=True))
    probs_low = jnp.exp(scores - log_total).astype(jnp.bfloat16)
    value_heads = value_rows.reshape(seq_count, value_rows.shape[1], head_count, head_size)
    context = jnp.einsum(
        "shqk,skhd->sqhd", probs_low, value_heads, preferred_element_type=jnp.float32
    )
    return (context.reshape(seq_count * length, inner_width), log_total)


def attn_backward(queries, key_rows, value_rows, key_valid, head_count, log_total, context_grad):
    seq_count, length, inner_width = queries.shape
    other_length = key_rows.shape[1]
    head_size = inner_width // head_count
    score_scale = 1.0 / math.sqrt(head_size)
    attn_probs = jnp.exp(scores_of(queries, key_rows, key_valid, head_count) - log_total)
    probs_low = attn_probs.astype(jnp.bfloat16)
    query_heads = queries.reshape(seq_count, length, head_count, head_size)
    key_heads = key_rows.reshape(seq_count, other_length, head_count, head_size)
    value_heads = value_rows.reshape(seq_count, other_length, head_count, head_size)
    grad_heads = context_grad.reshape(seq_count, length, head_count, head_size)
    grad_probs = jnp.einsum(
        "sqhd,skhd->shqk", grad_heads, value_heads, preferred_element_type=jnp.float32
    )
    grad_values = jnp.einsum(
        "shqk,sqhd->skhd", probs_low, grad_heads, preferred_element_type=jnp.float32
    )
    grad_scores = attn_probs * (
        grad_probs - jnp.sum(attn_probs * grad_probs, axis=-1, keepdims=True)
    )
    scores_low = grad_scores.astype(jnp.bfloat16)
    grad_queries = (
        jnp.einsum("shqk,skhd->sqhd", scores_low, key_heads, preferred_element_type=jnp.float32)
        * score_scale
    )
    grad_keys = (
        jnp.einsum("shqk,sqhd->skhd", scores_low, query_heads, preferred_element_type=jnp.float32)
        * score_scale
    )
    return (
        grad_queries.reshape(seq_count * length, inner_width),
        grad_keys.reshape(seq_count * other_length, inner_width),
        grad_values.reshape(seq_count * other_length, inner_width),
    )


def block_forward(inputs_low, residual, partner_low, params, key_valid, head_count):
    (
        query_weight,
        query_bias,
        key_weight,
        value_weight,
        value_bias,
        out_weight,
        out_bias,
        gain_one,
        shift_one,
        up_weight,
        up_bias,
        down_weight,
        down_bias,
        gain_two,
        shift_two,
    ) = params
    seq_count, length, model_width = inputs_low.shape
    other_length = partner_low.shape[1]
    flat_inputs = inputs_low.reshape(seq_count * length, model_width)
    flat_partner = partner_low.reshape(seq_count * other_length, partner_low.shape[2])
    queries = (product(flat_inputs, query_weight) + query_bias).astype(jnp.bfloat16)
    key_rows = product(flat_partner, key_weight).astype(jnp.bfloat16)
    value_rows = (product(flat_partner, value_weight) + value_bias).astype(jnp.bfloat16)
    inner_width = queries.shape[1]
    context, log_total = attn_forward(
        queries.reshape(seq_count, length, inner_width),
        key_rows.reshape(seq_count, other_length, inner_width),
        value_rows.reshape(seq_count, other_length, inner_width),
        key_valid,
        head_count,
    )
    context_low = context.astype(jnp.bfloat16)
    first_in = residual + (product(context_low, out_weight) + out_bias)
    first = layer_norm(first_in, gain_one.astype(jnp.float32), shift_one.astype(jnp.float32))
    first_low = first.astype(jnp.bfloat16)
    up_values = product(first_low, up_weight) + up_bias
    active_low = gelu_exact(up_values).astype(jnp.bfloat16)
    second_in = first + (product(active_low, down_weight) + down_bias)
    second = layer_norm(second_in, gain_two.astype(jnp.float32), shift_two.astype(jnp.float32))
    kept = (
        queries,
        key_rows,
        value_rows,
        log_total,
        context_low,
        first_in,
        first_low,
        up_values,
        active_low,
        second_in,
    )
    return (second, kept)


def block_backward(grad_second, kept, inputs_low, partner_low, params, key_valid, head_count):
    (
        query_weight,
        query_bias,
        key_weight,
        value_weight,
        value_bias,
        out_weight,
        out_bias,
        gain_one,
        shift_one,
        up_weight,
        up_bias,
        down_weight,
        down_bias,
        gain_two,
        shift_two,
    ) = params
    (
        queries,
        key_rows,
        value_rows,
        log_total,
        context_low,
        first_in,
        first_low,
        up_values,
        active_low,
        second_in,
    ) = kept
    seq_count, length, model_width = inputs_low.shape
    other_length = partner_low.shape[1]
    inner_width = queries.shape[1]
    flat_inputs = inputs_low.reshape(seq_count * length, model_width)
    flat_partner = partner_low.reshape(seq_count * other_length, partner_low.shape[2])
    norm_two = jax.vjp(
        layer_norm, second_in, gain_two.astype(jnp.float32), shift_two.astype(jnp.float32)
    )[1]
    grad_second_in, grad_gain_two, grad_shift_two = norm_two(grad_second)
    branch_low = grad_second_in.astype(jnp.bfloat16)
    grad_down = product_tn(active_low, branch_low)
    grad_active = product_nt(branch_low, down_weight)
    gelu_back = jax.vjp(gelu_exact, up_values)[1]
    up_low = gelu_back(grad_active)[0].astype(jnp.bfloat16)
    grad_up = product_tn(first_low, up_low)
    grad_first = grad_second_in + product_nt(up_low, up_weight)
    norm_one = jax.vjp(
        layer_norm, first_in, gain_one.astype(jnp.float32), shift_one.astype(jnp.float32)
    )[1]
    grad_first_in, grad_gain_one, grad_shift_one = norm_one(grad_first)
    out_low = grad_first_in.astype(jnp.bfloat16)
    grad_out = product_tn(context_low, out_low)
    context_grad = product_nt(out_low, out_weight).astype(jnp.bfloat16)
    grad_queries, grad_keys, grad_values = attn_backward(
        queries.reshape(seq_count, length, inner_width),
        key_rows.reshape(seq_count, other_length, inner_width),
        value_rows.reshape(seq_count, other_length, inner_width),
        key_valid,
        head_count,
        log_total,
        context_grad,
    )
    query_low = grad_queries.astype(jnp.bfloat16)
    key_low = grad_keys.astype(jnp.bfloat16)
    value_low = grad_values.astype(jnp.bfloat16)
    grads = [
        product_tn(flat_inputs, query_low),
        column_sums(query_low),
        product_tn(flat_partner, key_low),
        product_tn(flat_partner, value_low),
        column_sums(value_low),
        grad_out,
        column_sums(out_low),
        grad_gain_one,
        grad_shift_one,
        grad_up,
        column_sums(up_low),
        grad_down,
        column_sums(branch_low),
        grad_gain_two,
        grad_shift_two,
    ]
    grad_inputs = product_nt(query_low, query_weight)
    grad_partner = product_nt(key_low, key_weight) + product_nt(value_low, value_weight)
    return (grad_first_in, grad_inputs, grad_partner, grads)


def stream_dims(text_side):
    if text_side:
        return (DT, DI, FT, LT, LI, HT)
    return (DI, DT, FI, LI, LT, HI)


def count_masks(text_side, text_lengths, region_counts, own_length, other_length):
    own_count, other_count = (
        (text_lengths, region_counts) if text_side else (region_counts, text_lengths)
    )
    own_valid = jnp.arange(own_length, dtype=jnp.int32)[None, :] < own_count[:, None]
    other_valid = jnp.arange(other_length, dtype=jnp.int32)[None, :] < other_count[:, None]
    return (own_valid, other_valid)


def co_forward(text_side, with_kept, states_box, partner_box, co_full, text_lengths, region_counts):
    model_width, other_width, hidden, own_length, other_length, head_count = stream_dims(text_side)
    seq_count = states_box.shape[0]
    own_valid, other_valid = count_masks(
        text_side, text_lengths, region_counts, own_length, other_length
    )
    params = unpack(co_full, shapes(model_width, other_width, DC, hidden))
    inputs_low = states_box.reshape(seq_count, own_length, model_width)
    partner_low = partner_box.reshape(seq_count, other_length, other_width)
    residual = inputs_low.reshape(seq_count * own_length, model_width).astype(jnp.float32)
    second, kept = block_forward(inputs_low, residual, partner_low, params, other_valid, HC)
    return second.reshape(states_box.shape)


def self_section(text_side, first_box, grad_box, self_full, text_lengths, region_counts):
    model_width, other_width, hidden, own_length, other_length, head_count = stream_dims(text_side)
    seq_count = first_box.shape[0]
    own_valid, other_valid = count_masks(
        text_side, text_lengths, region_counts, own_length, other_length
    )
    params = unpack(self_full, shapes(model_width, model_width, model_width, hidden))
    residual = first_box.reshape(seq_count * own_length, model_width)
    inputs_low = residual.astype(jnp.bfloat16).reshape(seq_count, own_length, model_width)
    output, kept = block_forward(inputs_low, residual, inputs_low, params, own_valid, head_count)
    grad_rows = grad_box.reshape(seq_count * own_length, model_width).astype(jnp.float32)
    grad_resid, grad_inputs, grad_partner, grads = block_backward(
        grad_rows, kept, inputs_low, inputs_low, params, own_valid, head_count
    )
    grad_first = grad_resid + grad_inputs + grad_partner
    return (
        output.astype(jnp.bfloat16).reshape(grad_box.shape),
        grad_first.reshape(first_box.shape),
        pack(grads, self_full.shape[0]),
    )


def co_backward(text_side, states_box, partner_box, co_full, grad_box, text_lengths, region_counts):
    model_width, other_width, hidden, own_length, other_length, head_count = stream_dims(text_side)
    seq_count = states_box.shape[0]
    own_valid, other_valid = count_masks(
        text_side, text_lengths, region_counts, own_length, other_length
    )
    params = unpack(co_full, shapes(model_width, other_width, DC, hidden))
    inputs_low = states_box.reshape(seq_count, own_length, model_width)
    partner_low = partner_box.reshape(seq_count, other_length, other_width)
    residual = inputs_low.reshape(seq_count * own_length, model_width).astype(jnp.float32)
    kept = block_forward(inputs_low, residual, partner_low, params, other_valid, HC)[1]
    grad_rows = grad_box.reshape(seq_count * own_length, model_width)
    grad_resid, grad_inputs, grad_partner, grads = block_backward(
        grad_rows, kept, inputs_low, partner_low, params, other_valid, HC
    )
    own_grad = (grad_resid + grad_inputs).reshape(states_box.shape)
    sent_grad = grad_partner.astype(jnp.bfloat16).reshape(states_box.shape)
    return (own_grad, sent_grad, pack(grads, co_full.shape[0]))


def again_backward(
    text_side, states_box, partner_box, co_full, grad_box, text_lengths, region_counts
):
    return co_backward(
        text_side, states_box, partner_box, co_full, grad_box, text_lengths, region_counts
    )


def body(states, out_grad, co_params, self_params, text_lengths, region_counts):
    own_states = states[0]
    own_cotangent = out_grad[0]
    text_stream = lax.axis_index("stream") == 0
    partner_states = from_partner(own_states, "stream", 0)
    co_full = lax.all_gather(co_params[0].astype(jnp.bfloat16), "dp", axis=0, tiled=True)
    first_box = lax.cond(
        text_stream,
        functools.partial(co_forward, True, False),
        functools.partial(co_forward, False, False),
        own_states,
        partner_states,
        co_full,
        text_lengths,
        region_counts,
    )
    self_full = lax.all_gather(self_params[0].astype(jnp.bfloat16), "dp", axis=0, tiled=True)
    output_box, grad_first, self_flat = lax.cond(
        text_stream,
        functools.partial(self_section, True),
        functools.partial(self_section, False),
        first_box,
        own_cotangent,
        self_full,
        text_lengths,
        region_counts,
    )
    co_back = lax.all_gather(co_params[0].astype(jnp.bfloat16), "dp", axis=0, tiled=True)
    own_grad, sent_grad, co_flat = lax.cond(
        text_stream,
        functools.partial(again_backward, True),
        functools.partial(again_backward, False),
        own_states,
        partner_states,
        co_back,
        grad_first,
        text_lengths,
        region_counts,
    )
    returned = from_partner(sent_grad, "stream", 0)
    states_grad = own_grad + returned.astype(jnp.float32)
    co_rows, self_rows = (
        lax.psum_scatter(as_rows(co_flat), "dp", scatter_dimension=0, tiled=True),
        lax.psum_scatter(as_rows(self_flat), "dp", scatter_dimension=0, tiled=True),
    )
    co_shard = co_rows.reshape(-1)
    self_shard = self_rows.reshape(-1)
    return (output_box[None], states_grad[None], co_shard[None], self_shard[None])


def solution(mesh):
    in_specs = (
        P("stream", "dp", None, None),
        P("stream", "dp", None, None),
        P("stream", "dp"),
        P("stream", "dp"),
        P("dp"),
        P("dp"),
    )
    out_specs = (
        P("stream", "dp", None, None),
        P("stream", "dp", None, None),
        P("stream", "dp"),
        P("stream", "dp"),
    )
    return jax.shard_map(body, mesh=mesh, in_specs=in_specs, out_specs=out_specs, check_vma=False)
```

profile of v0, /device:TPU:9, one launch (start us, length us, event | category | flops | bytes accessed | tf_op | source)
XLA Modules:
  0.0 2425.3 jit_solution(15901668835895541208)
XLA Ops:
  17.4 139.6 %all-gather.5.cloned.1.call-done = bf16[1,7088128]{1,0:T(2,128)(2,1)} async-done(((bf16[1,443008]{1,0:T(2,128)(2,1)}), bf16[1,7088128]{1,0:T(2,128)(2,1)}) %all-gather.5.cloned.1.call-update) | async-done | bytes 14176272 | tf_op jit(solution)/shard_map/all_gather | solution.py:398
  157.0 300.8 %reduce.10 = bf16[7088128]{0:T(1024)(128)(2,1)} reduce(bf16[1,7088128]{1,0:T(2,128)(2,1)} %all-gather.5.cloned.1.call-done, bf16[]{:T(256)} %constant.526), dimensions={0}, to_apply=%all-gather.reduce_sub_computation | reduce | bytes 28352514 | tf_op jit(solution)/shard_map/all_gather | solution.py:398
  457.8 355.9 %reduce.11 = bf16[8398848]{0:T(1024)(128)(2,1)} reduce(bf16[1,8398848]{1,0:T(2,128)(2,1)} %all-gather.7.cloned.1.call-done, bf16[]{:T(256)} %constant.526), dimensions={0}, to_apply=%all-gather.1.reduce_sub_computation | reduce | bytes 33595392 | tf_op jit(solution)/shard_map/all_gather | solution.py:387
  813.6 72.7 %conditional.3 = (f32[2,96,1024]{2,1,0:T(8,128)S(1)}) conditional(s32[]{:T(128)} %convert_element_type.690, (bf16[1,2,96,1024]{3,2,1,0:T(8,128)(2,1)S(1)}, bf16[2,96,1024]{2,1,0:T(8,128)(2,1)}, bf16[8398848]{0:T(1024)(128)(2,1)}, s32[2]{0:T(128)S(1)}) %tuple.197, (bf16[1,2,96,1024]{3,2,1,0:T(8,128)(2,1)S(1)}, bf16[2,96,1024]{2,1,0:T(8,128)(2,1)}, ...), branch_computations={%region_0.7_spmd, %region_7.14_spmd} | conditional | flops 4186972416 | bytes 121558624 | solution.py:388
  823.1 4.5 fusion.413
  844.8 9.2 fusion.415
  853.9 8.2 reshape.985
  862.2 9.6 reshape.986
  872.5 13.0 fusion.418
  886.3 443.9 %conditional.4 = (f32[2,96,1024]{2,1,0:T(8,128)S(1)}, f32[7088128]{0:T(1024)}, bf16[1,2,96,1024]{3,2,1,0:T(8,128)(2,1)}) conditional(s32[]{:T(128)} %convert_element_type.690, (bf16[1,2,96,1024]{3,2,1,0:T(8,128)(2,1)S(1)}, bf16[7088128]{0:T(1024)(128)(2,1)}, f32[2,96,1024]{2,1,0:T(8,128)S(1)}, s32[2]{0:T(128)}) %tuple.195, ...), branch_computations={%region_14.35_spmd, %region_35.56_spmd} | conditional | flops 11262292992 | bytes 481696000 | solution.py:399
  903.0 4.5 fusion.427
  929.6 9.2 fusion.426
  938.8 8.2 reshape.1008
  947.7 11.7 multiply_convert_fusion.2
  959.5 9.2 reshape.1009
  981.2 5.8 convert_reduce_fusion.6
  1027.2 21.5 dynamic-update-slice.17
  1059.6 21.4 dynamic-update-slice.18
  1087.5 21.3 dynamic-update-slice.20
  1115.7 5.7 copy.242
  1121.5 80.5 %dynamic-update-slice.24 = f32[7087104]{0:T(1024)} dynamic-update-slice(f32[7087104]{0:T(1024)} %constant_dynamic-update-slice_fusion.19, f32[2359296]{0:T(1024)} %bitcast.519, s32[]{} %constant.552) | dynamic-update-slice | bytes 18874372 | tf_op jit(solution)/shard_map/cond
  1203.3 6.4 fusion.442
  1209.7 10.7 reshape.1017
  1220.5 80.5 %dynamic-update-slice.26 = f32[7087104]{0:T(1024)} dynamic-update-slice(f32[7087104]{0:T(1024)} %constant_dynamic-update-slice_fusion.18, f32[2359296]{0:T(1024)} %reshape.1017, s32[]{} %constant.554) | dynamic-update-slice | bytes 18874372 | tf_op jit(solution)/shard_map/cond
  1304.8 21.7 pad.13
  1330.3 300.0 %fusion.1 = f32[3472,128]{1,0:T(8,128)} fusion(f32[55376,128]{1,0:T(8,128)} %bitcast.52), kind=kCustom, calls=%all-reduce-scatter.1 | all-reduce-scatter fusion | flops 7110657 | bytes 30130688
  1631.8 4.4 collective-permute-start.3
  1636.2 381.4 %conditional.5 = (f32[2,96,1024]{2,1,0:T(8,128)}, bf16[2,96,1024]{2,1,0:T(8,128)(2,1)}, f32[8398848]{0:T(1024)}) conditional(s32[]{:T(128)} %convert_element_type.690, (f32[2,96,1024]{2,1,0:T(8,128)S(1)}, bf16[8398848]{0:T(1024)(128)(2,1)}, bf16[1,2,96,1024]{3,2,1,0:T(8,128)(2,1)S(1)}, bf16[2,96,1024]{2,1,0:T(8,128)(2,1)}, ...), branch_computations={%region_56.77_spmd, %region_77.98_spmd} | conditional | flops 12466846720 | bytes 563851712 | solution.py:410
  1653.2 4.8 fusion.437
  1681.1 9.1 fusion.436
  1690.2 8.2 reshape.1038
  1699.2 11.6 multiply_convert_fusion.6
  1710.7 9.6 reshape.1039
  1730.0 5.7 convert_reduce_fusion.16
  1758.6 5.4 copy.208
  1774.4 5.4 copy.209
  1798.3 5.8 copy.268
  1804.1 80.9 %dynamic-update-slice.54 = f32[8398336]{0:T(1024)} dynamic-update-slice(f32[8398336]{0:T(1024)} %constant_dynamic-update-slice_fusion.44, f32[2359296]{0:T(1024)} %bitcast.520, s32[]{} %constant.582) | dynamic-update-slice | bytes 18874372 | tf_op jit(solution)/shard_map/cond
  1886.4 5.1 fusion.443
  1891.5 10.8 reshape.1048
  1902.3 80.2 %dynamic-update-slice.56 = f32[8398336]{0:T(1024)} dynamic-update-slice(f32[8398336]{0:T(1024)} %constant_dynamic-update-slice_fusion.43, f32[2359296]{0:T(1024)} %reshape.1048, s32[]{} %constant.584) | dynamic-update-slice | bytes 18874372 | tf_op jit(solution)/shard_map/cond
  1986.4 26.1 %pad.15 = f32[8398848]{0:T(1024)} pad(f32[8398336]{0:T(1024)} %constant_dynamic-update-slice_fusion.40, f32[]{:T(128)} %constant.423.clone), padding=0_512 | pad | bytes 67188736 | tf_op jit(solution)/shard_map/cond/branch_1_fun/jit(_pad)/pad | solution.py:61
  2017.7 352.5 %fusion = f32[4112,128]{1,0:T(8,128)S(1)} fusion(f32[65616,128]{1,0:T(8,128)} %bitcast.518), kind=kCustom, calls=%all-reduce-scatter | all-reduce-scatter fusion | flops 8421377 | bytes 35701248
  2370.2 4.4 collective-permute-start.2
  2374.6 6.7 concatenate.13
  2382.9 11.8 copy.554
  2394.7 5.7 concatenate.12
  2402.2 13.8 copy.553
  (447 shorter events, 257.2 us)
Async XLA Ops:
  7.2 149.8 %all-gather.5.cloned.1.call-start = ((), (), s32[]{:S(2)}) async-start(), calls=%async_computation | async-start | bytes 30124544 | tf_op jit(solution)/shard_map/all_gather | solution.py:398
  11.6 446.2 %all-gather.7.cloned.1.call-start = ((), (), s32[]{:S(2)}) async-start(), calls=%async_computation.1 | async-start | bytes 35695104 | tf_op jit(solution)/shard_map/all_gather | solution.py:387
  14.9 798.8 %collective-permute-start = (bf16[2,96,1024]{2,1,0:T(8,128)(2,1)S(1)}, bf16[2,96,1024]{2,1,0:T(8,128)(2,1)}, u32[]{:S(2)}, u32[]{:S(2)}) collective-permute-start(bf16[2,96,1024]{2,1,0:T(8,128)(2,1)S(1)} %bitcast.548), channel_id=1, source_target_pairs={{0,16},{16,0},{1,17},{17,1},{2,18},{18,2},{3,19},{19,3},{4,20},{20... | collective-permute-start | bytes 1179656 | tf_op jit(solution)/shard_map/ppermute | solution.py:26
  457.8 355.9 %copy-start.220 = (s32[2]{0:T(128)S(1)}, s32[2]{0:T(128)}, u32[]{:S(2)}) copy-start(s32[2]{0:T(128)} %param.16) | copy-start | bytes 28
  813.6 72.7 %copy-start.12 = (bf16[1,2,96,1024]{3,2,1,0:T(8,128)(2,1)S(1)}, bf16[1,2,96,1024]{3,2,1,0:T(8,128)(2,1)}, u32[]{:S(2)}) copy-start(bf16[1,2,96,1024]{3,2,1,0:T(8,128)(2,1)} %param.13) | copy-start | bytes 1179652
  862.2 10.3 copy-start.210
  929.3 39.4 %copy-start.137 = (f32[256]{0:T(256)}, f32[256]{0:T(256)S(1)}, u32[]{:S(2)}) copy-start(f32[256]{0:T(256)S(1)} %broadcast_multiply_fusion.7) | copy-start | bytes 3076 | tf_op jit(solution)/shard_map/cond
  929.5 9.2 copy-start.186
  929.6 39.1 %copy-start.178 = (f32[256]{0:T(256)}, f32[256]{0:T(256)S(1)}, u32[]{:S(2)}) copy-start(f32[256]{0:T(256)S(1)} %fusion.277) | copy-start | bytes 3076 | tf_op jit(solution)/shard_map/cond
  959.5 9.2 copy-start.204
  977.8 9.2 slice-start
  1059.6 21.4 copy-start.134
  1059.6 22.7 copy-start.63
  1059.6 22.7 copy-start.69
  1087.5 21.3 copy-start.170
  1087.5 22.6 copy-start.214
  1087.5 23.9 copy-start.213
  1087.5 25.2 %copy-start.130 = (f32[768]{0:T(1024)S(1)}, f32[768]{0:T(1024)}, u32[]{:S(2)}) copy-start(f32[768]{0:T(1024)} %get-tuple-element.243) | copy-start | bytes 9220 | tf_op jit(solution)/shard_map/cond
  1087.5 25.2 %copy-start.132 = (f32[768]{0:T(1024)S(1)}, f32[768]{0:T(1024)}, u32[]{:S(2)}) copy-start(f32[768]{0:T(1024)} %get-tuple-element.242) | copy-start | bytes 9220 | tf_op jit(solution)/shard_map/cond
  1087.5 25.2 %copy-start.139 = (f32[256]{0:T(256)S(1)}, f32[256]{0:T(256)}, u32[]{:S(2)}) copy-start(f32[256]{0:T(256)} %copy-done.137) | copy-start | bytes 3076 | tf_op jit(solution)/shard_map/cond
  1087.5 25.2 %copy-start.180 = (f32[256]{0:T(256)S(1)}, f32[256]{0:T(256)}, u32[]{:S(2)}) copy-start(f32[256]{0:T(256)} %copy-done.178) | copy-start | bytes 3076 | tf_op jit(solution)/shard_map/cond
  1121.5 80.5 %copy-start.184 = (f32[3072]{0:T(1024)S(1)}, f32[3072]{0:T(1024)}, u32[]{:S(2)}) copy-start(f32[3072]{0:T(1024)} %get-tuple-element.132) | copy-start | bytes 36868 | tf_op jit(solution)/shard_map/cond
  1121.5 81.8 %copy-start.87 = (bf16[256,768]{1,0:T(8,128)(2,1)S(1)}, bf16[256,768]{1,0:T(8,128)(2,1)}, u32[]{:S(2)}) copy-start(bf16[256,768]{1,0:T(8,128)(2,1)} %copy-done.86) | copy-start | bytes 1179652 | tf_op jit(solution)/shard_map/cond
  1220.5 80.5 %copy-start.162 = (f32[768]{0:T(1024)S(1)}, f32[768]{0:T(1024)}, u32[]{:S(2)}) copy-start(f32[768]{0:T(1024)} %get-tuple-element.130) | copy-start | bytes 9220 | tf_op jit(solution)/shard_map/cond
  1220.5 81.8 %copy-start.157 = (f32[768]{0:T(1024)S(1)}, f32[768]{0:T(1024)}, u32[]{:S(2)}) copy-start(f32[768]{0:T(1024)} %get-tuple-element.103) | copy-start | bytes 9220 | tf_op jit(solution)/shard_map/cond
  1220.5 83.0 %copy-start.156 = (f32[768]{0:T(1024)S(1)}, f32[768]{0:T(1024)}, u32[]{:S(2)}) copy-start(f32[768]{0:T(1024)} %get-tuple-element.107) | copy-start | bytes 9220 | tf_op jit(solution)/shard_map/cond
  1304.8 21.8 copy-start.8
  1304.8 21.8 copy-start.54
  1304.8 22.3 copy-start.43
  1304.8 22.3 copy-start.65
  1304.8 22.3 copy-start.196
  1330.2 306.0 %copy-start.11 = (bf16[1,2,96,1024]{3,2,1,0:T(8,128)(2,1)S(1)}, bf16[1,2,96,1024]{3,2,1,0:T(8,128)(2,1)}, u32[]{:S(2)}) copy-start(bf16[1,2,96,1024]{3,2,1,0:T(8,128)(2,1)} %param.12) | copy-start | bytes 1179652
  1330.3 306.0 %copy-start.221 = (s32[2]{0:T(128)S(1)}, s32[2]{0:T(128)}, u32[]{:S(2)}) copy-start(s32[2]{0:T(128)} %param.16) | copy-start | bytes 28
  1631.8 742.8 %collective-permute-start.3 = (f32[165,128]{1,0:T(8,128)}, f32[165,128]{1,0:T(8,128)}, u32[]{:S(2)}, u32[]{:S(2)}) collective-permute-start(f32[165,128]{1,0:T(8,128)} %slice.505), channel_id=1, source_target_pairs={{0,1},{1,2},{2,3},{3,4},{4,5},{5,6},{6,7},{7,8},{8,9},{9,10},{10,1... | collective-permute-start | bytes 253448
  1653.2 11.4 copy-start.82
  1680.8 39.6 %copy-start.27 = (f32[256,768]{1,0:T(8,128)}, f32[256,768]{1,0:T(8,128)S(1)}, u32[]{:S(2)}) copy-start(f32[256,768]{1,0:T(8,128)S(1)} %get-tuple-element.313) | copy-start | bytes 2359300 | tf_op jit(solution)/shard_map/cond
  1680.8 18.3 copy-start.140
  1681.1 18.1 copy-start.181
  1804.1 81.0 %copy-start.185 = (f32[3072]{0:T(1024)S(1)}, f32[3072]{0:T(1024)}, u32[]{:S(2)}) copy-start(f32[3072]{0:T(1024)} %get-tuple-element.156) | copy-start | bytes 36868 | tf_op jit(solution)/shard_map/cond
  1804.1 82.3 %copy-start.79 = (bf16[256,3072]{1,0:T(8,128)(2,1)S(1)}, bf16[256,3072]{1,0:T(8,128)(2,1)}, u32[]{:S(2)}) copy-start(bf16[256,3072]{1,0:T(8,128)(2,1)} %get-tuple-element.164) | copy-start | bytes 4718596 | tf_op jit(solution)/shard_map/cond
  1804.1 82.3 %copy-start.89 = (bf16[256,768]{1,0:T(8,128)(2,1)S(1)}, bf16[256,768]{1,0:T(8,128)(2,1)}, u32[]{:S(2)}) copy-start(bf16[256,768]{1,0:T(8,128)(2,1)} %copy-done.88) | copy-start | bytes 1179652 | tf_op jit(solution)/shard_map/cond
  1902.3 80.3 %copy-start.163 = (f32[768]{0:T(1024)S(1)}, f32[768]{0:T(1024)}, u32[]{:S(2)}) copy-start(f32[768]{0:T(1024)} %get-tuple-element.154) | copy-start | bytes 9220 | tf_op jit(solution)/shard_map/cond
  1902.3 81.5 %copy-start.160 = (f32[768]{0:T(1024)S(1)}, f32[768]{0:T(1024)}, u32[]{:S(2)}) copy-start(f32[768]{0:T(1024)} %get-tuple-element.114) | copy-start | bytes 9220 | tf_op jit(solution)/shard_map/cond
  1902.3 82.8 %copy-start.158 = (f32[768]{0:T(1024)S(1)}, f32[768]{0:T(1024)}, u32[]{:S(2)}) copy-start(f32[768]{0:T(1024)} %get-tuple-element.118) | copy-start | bytes 9220 | tf_op jit(solution)/shard_map/cond
  1986.4 26.1 %copy-start.1 = (bf16[1024,1024]{1,0:T(8,128)(2,1)S(1)}, bf16[1024,1024]{1,0:T(8,128)(2,1)}, u32[]{:S(2)}) copy-start(bf16[1024,1024]{1,0:T(8,128)(2,1)} %slice.495) | copy-start | bytes 6291460 | tf_op jit(solution)/shard_map/cond
  1986.4 27.0 %copy-start.58 = (bf16[2,96,8,128]{3,2,1,0:T(8,128)(2,1)S(1)}, bf16[2,96,8,128]{3,2,1,0:T(8,128)(2,1)}, u32[]{:S(2)}) copy-start(bf16[2,96,8,128]{3,2,1,0:T(8,128)(2,1)} %copy-done.57) | copy-start | bytes 1179652 | tf_op jit(solution)/shard_map/cond
  2370.2 24.5 %collective-permute-start.2 = (f32[165,128]{1,0:T(8,128)S(1)}, f32[165,128]{1,0:T(8,128)S(1)}, u32[]{:S(2)}, u32[]{:S(2)}) collective-permute-start(f32[165,128]{1,0:T(8,128)S(1)} %slice.504), channel_id=1, source_target_pairs={{0,1},{1,2},{2,3},{3,4},{4,5},{5,6},{6,7},{7,8},{8,9},{9,10},{10,1... | collective-permute-start | bytes 253448
  2374.5 41.5 %collective-permute-start.1 = (bf16[2,96,1024]{2,1,0:T(8,128)(2,1)}, bf16[2,96,1024]{2,1,0:T(8,128)(2,1)S(1)}, u32[]{:S(2)}, u32[]{:S(2)}) collective-permute-start(bf16[2,96,1024]{2,1,0:T(8,128)(2,1)} %get-tuple-element.95), channel_id=1, source_target_pairs={{0,16},{16,0},{1,17},{17,1},{2,18},{18,2},{3,19},{19,3},{4,20},{20... | collective-permute-start | bytes 1179656 | tf_op jit(solution)/shard_map/ppermute | solution.py:26
  (76 other events, 286.6 us)
Sparse Core Ops, SparseCore 0:
  11.7 145.2 all-gather.4
  159.1 168.2 all-gather.6
where the time goes:
time: 2470 us; the launch traced here: 2430 us
  local copies, waits for them, and re-layouts  757 us (31%)
  other arithmetic  690 us (28%)
  blocking collectives  653 us (26%)
  waiting for transfers between devices  140 us (6%)
  matrix products  136 us (6%)
  loops' own time  25.9 us (1%)
    unnamed x2, blocking collectives  653 us
    cond x262, local copies, waits for them, and re-layouts  450 us
    all_gather x1, other arithmetic, body(): lax.all_gather(co_params[0].astype(jnp.bfloat16), 'dp', axis=0, tiled=True)  356 us
    all_gather x1, other arithmetic, body(): lax.all_gather(self_params[0].astype(jnp.bfloat16), 'dp', axis=0, tiled=T...  301 us
    all_gather x1, waiting for transfers between devices, body(): lax.all_gather(self_params[0].astype(jnp.bfloat16), 'dp', axis=0, tiled=T...  140 us
    reshape x12, local copies, waits for them, and re-layouts, unpack(): pieces.append(flat_values[offset:offset + piece_count].reshape(piece_shape))  68.2 us
    dot_general x17, matrix products, product(): return jnp.dot(left_side, right_side, preferred_element_type=jnp.float32)  66.4 us
    slice x14, local copies, waits for them, and re-layouts, unpack(): pieces.append(flat_values[offset:offset + piece_count].reshape(piece_shape))  66.3 us
  transfers between devices with their start and end apart: 6, of which 1 were waited for; matrix products, arithmetic and copies ran while one was open for 59% of the time, Pallas kernels for 0%

commit v1 on v0

v1 whole, which is shorter than its diff:
```python
import functools
import math

import jax
import jax.numpy as jnp
import numpy as np
from jax import lax
from jax.experimental import pallas as pl
from jax.experimental.pallas import tpu as pltpu
from jax.sharding import PartitionSpec as P


MESH_ID = pl.DeviceIdType.MESH
UNITS = 6


def place(line):
    d = lax.axis_index("dp")
    return d // 4, lax.rem(d // 2, 2), lax.rem(d, 2)


def greet(line):
    z, x, c = place(line)
    s = lax.axis_index("stream")
    barrier = pltpu.get_barrier_semaphore()

    def signal(zz, xx, cc):
        pl.semaphore_signal(barrier, inc=1, device_id=(s, (zz * 2 + xx) * 2 + cc), device_id_type=MESH_ID)

    signal(z, 1 - x, c)
    signal(z, x, 1 - c)

    @pl.when(z > 0)
    def _():
        signal(z - 1, x, c)

    @pl.when(z < line - 1)
    def _():
        signal(z + 1, x, c)

    pl.semaphore_wait(barrier, 2 + jnp.minimum(z, 1) + jnp.minimum(line - 1 - z, 1))


def gather_kernel(line, own, out, up_s, dn_s, z_r, x_s, x_r, c_s, c_r, l_s):
    z, x, c = place(line)
    s = lax.axis_index("stream")
    n = own.shape[0] // UNITS
    greet(line)

    def piece(u):
        return pl.ds(u * n, n)

    def copy(src, dst, send, recv, zz, xx, cc):
        return pltpu.make_async_remote_copy(
            src_ref=src, dst_ref=dst, send_sem=send, recv_sem=recv,
            device_id=(s, (zz * 2 + xx) * 2 + cc), device_id_type=MESH_ID)

    def block_of(v):
        return jnp.where(v == UNITS, 1 - x, x), jnp.minimum(v, UNITS - 1)

    def z_copy(zo, v, up, mine=False):
        xb, u = block_of(v)
        place_ = out.at[zo, xb, c, piece(u)]
        src = own.at[piece(u)] if mine else place_
        k = zo * (UNITS + 1) + v
        return copy(src, place_, (up_s if up else dn_s).at[k], z_r.at[k], (z + 1 if up else z - 1), x, c)

    def x_copy(zo, u, mine=False, arriving=False):
        xb = 1 - x if arriving else x
        place_ = out.at[zo, xb, c, piece(u)]
        src = own.at[piece(u)] if mine else place_
        k = zo * UNITS + u
        return copy(src, place_, x_s.at[k], x_r.at[k], z, 1 - x, c)

    def c_copy(zo, xb, u, mine=False):
        place_ = out.at[zo, xb, c, piece(u)]
        src = own.at[piece(u)] if mine else place_
        return copy(src, place_, c_s.at[(zo * 2 + xb) * UNITS + u], c_r, z, x, 1 - c)

    local = pltpu.make_async_copy(own, out.at[z, x, c], l_s)
    local.start()
    has_up, has_dn = z < line - 1, z > 0

    def send_z(zo, v, mine=False):
        @pl.when(has_up)
        def _():
            z_copy(zo, v, True, mine).start()

        @pl.when(has_dn)
        def _():
            z_copy(zo, v, False, mine).start()

    x_copy(z, UNITS - 1, True).start()
    for u in range(UNITS - 1):
        x_copy(z, u, True).start()
        send_z(z, u, True)
    send_z(z, UNITS - 1, True)
    for u in range(UNITS):
        c_copy(z, x, u, True).start()
    x_copy(z, UNITS - 1, arriving=True).wait_recv()
    send_z(z, UNITS)
    c_copy(z, 1 - x, UNITS - 1).start()

    per = UNITS + 1
    slots = per * (line - 1)
    lag = per

    def x_arrival(zo, u):
        x_copy(zo, u, arriving=True).wait_recv()
        c_copy(zo, 1 - x, u).start()

    def slot(t, carry):
        h, v = t // per, lax.rem(t, per)
        xb, u = block_of(v)

        @pl.when(z > h)
        def _():
            zo = z - 1 - h
            z_copy(zo, v, True).wait_recv()

            @pl.when(has_up)
            def _():
                z_copy(zo, v, True).start()

            @pl.when(v < UNITS - 1)
            def _():
                x_copy(zo, u).start()

            c_copy(zo, xb, u).start()

        @pl.when(z + h < line - 1)
        def _():
            zo = z + 1 + h
            z_copy(zo, v, False).wait_recv()

            @pl.when(has_dn)
            def _():
                z_copy(zo, v, False).start()

            @pl.when(v < UNITS - 1)
            def _():
                x_copy(zo, u).start()

            c_copy(zo, xb, u).start()

        late(t - lag)
        return carry

    def late(t):
        @pl.when(jnp.logical_and(t < 0, t + per < UNITS - 1))
        def _():
            x_arrival(z, t + per)

        h, v = t // per, lax.rem(t, per)

        @pl.when(jnp.logical_and(t >= 0, v < UNITS - 1))
        def _():
            @pl.when(z > h)
            def _():
                x_arrival(z - 1 - h, v)

            @pl.when(z + h < line - 1)
            def _():
                x_arrival(z + 1 + h, v)

    lax.fori_loop(0, slots, slot, 0)

    def rest(t, carry):
        late(t)
        return carry

    lax.fori_loop(slots - lag, slots, rest, 0)

    pltpu.make_async_remote_copy(
        src_ref=out.at[:, :, c], dst_ref=out.at[:, :, 1 - c], send_sem=l_s, recv_sem=c_r,
        device_id=(s, (z * 2 + x) * 2 + 1 - c), device_id_type=MESH_ID).wait_recv()
    local.wait()

    def sent(zo, carry):
        for v in range(per):
            @pl.when(jnp.logical_and(has_up, zo <= z))
            def _():
                z_copy(zo, v, True).wait_send()

            @pl.when(jnp.logical_and(has_dn, zo >= z))
            def _():
                z_copy(zo, v, False).wait_send()
        for u in range(UNITS - 1):
            x_copy(zo, u).wait_send()
        @pl.when(zo == z)
        def _():
            x_copy(zo, UNITS - 1).wait_send()
        for xb in range(2):
            for u in range(UNITS):
                c_copy(zo, xb, u).wait_send()
        return carry

    lax.fori_loop(0, line, sent, 0)


def gather(own, line, cid, name):
    rows = own.shape[0]
    dma = pltpu.SemaphoreType.DMA
    per = UNITS + 1
    return pl.pallas_call(
        functools.partial(gather_kernel, line),
        out_shape=jax.ShapeDtypeStruct((line, 2, 2) + own.shape, own.dtype),
        in_specs=[pl.BlockSpec(memory_space=pl.ANY)],
        out_specs=pl.BlockSpec(memory_space=pl.ANY),
        scratch_shapes=[dma((line * per,)), dma((line * per,)), dma((line * per,)), dma((line * UNITS,)), dma((line * UNITS,)),
                        dma((line * 2 * UNITS,)), dma, dma],
        compiler_params=pltpu.CompilerParams(collective_id=cid, has_side_effects=True),
        name=name,
    )(own)


def scatter_kernel(line, lead, g, out, gv, cr, xr, ur, dr, l_s, c_s, c_r, x_s, x_r, u_s, u_r, d_s, d_r):
    z, x, c = place(line)
    s = lax.axis_index("stream")
    per = UNITS + 1
    n = gv.shape[2] // UNITS
    last = line - 1

    def piece(u):
        return pl.ds(u * n, n)

    def copy(src, dst, send, recv, zz, xx, cc):
        return pltpu.make_async_remote_copy(
            src_ref=src, dst_ref=dst, send_sem=send, recv_sem=recv,
            device_id=(s, (zz * 2 + xx) * 2 + cc), device_id_type=MESH_ID)

    def block_of(v):
        return jnp.where(v == 0, 1 - x, x), jnp.where(v < 2, UNITS - 1, v - 2)

    def local(zo, xb, u):
        return pltpu.make_async_copy(g.at[zo, xb, c, piece(u)], gv.at[zo, xb, piece(u)], l_s.at[(zo * 2 + xb) * UNITS + u])

    def c_copy(zo, xb, u):
        k = (zo * 2 + xb) * UNITS + u
        return copy(g.at[zo, xb, 1 - c, piece(u)], cr.at[zo, xb, piece(u)], c_s.at[k], c_r.at[k], z, x, 1 - c)

    def x_copy(zo, u):
        k = zo * UNITS + u
        return copy(gv.at[zo, 1 - x, piece(u)], xr.at[zo, piece(u)], x_s.at[k], x_r.at[k], z, 1 - x, c)

    def z_copy(to, v, up):
        xb, u = block_of(v)
        k = to * per + v
        dst, send, recv = (ur, u_s, u_r) if up else (dr, d_s, d_r)
        return copy(gv.at[to, xb, piece(u)], dst.at[to, pl.ds(v * n, n)], send.at[k], recv.at[k], (z + 1 if up else z - 1), x, c)

    def wide(value):
        return value.astype(jnp.float32)

    def both_cores(zo, xb, u):
        local(zo, xb, u).wait()
        c_copy(zo, xb, u).wait_recv()
        return wide(gv[zo, xb, piece(u)]) + wide(cr[zo, xb, piece(u)])

    def start_block(zo):
        for xb in (1 - x, x):
            for u in range(UNITS):
                local(zo, xb, u).start()

    def send_block(zo):
        for xb in (1 - x, x):
            for u in range(UNITS):
                c_copy(zo, xb, u).start()

    lax.fori_loop(0, line, lambda i, k: (start_block(i), k)[1], 0)
    greet(line)
    lax.fori_loop(0, line, lambda i, k: (send_block(i), k)[1], 0)

    def x_send(zo, u):
        gv[zo, 1 - x, piece(u)] = both_cores(zo, 1 - x, u).astype(gv.dtype)
        x_copy(zo, u).start()

    def z_send(to, v, up):
        xb, u = block_of(v)
        first = z == (0 if up else last)
        got = ur if up else dr

        @pl.when(v < 2)
        def _():
            total = both_cores(to, xb, u)

            @pl.when(first)
            def _():
                gv[to, xb, piece(u)] = total.astype(gv.dtype)

            @pl.when(jnp.logical_not(first))
            def _():
                z_copy(to, v, up).wait_recv()
                gv[to, xb, piece(u)] = (total + wide(got[to, pl.ds(v * n, n)])).astype(gv.dtype)

        @pl.when(v >= 2)
        def _():
            total = both_cores(to, xb, u)
            x_copy(to, u).wait_recv()
            total = total + wide(xr[to, piece(u)])

            @pl.when(first)
            def _():
                gv[to, xb, piece(u)] = total.astype(gv.dtype)

            @pl.when(jnp.logical_not(first))
            def _():
                z_copy(to, v, up).wait_recv()
                gv[to, xb, piece(u)] = (total + wide(got[to, pl.ds(v * n, n)])).astype(gv.dtype)

        z_copy(to, v, up).start()

    def stage(t, act):
        i = t - z
        to = last - i // per

        @pl.when(jnp.logical_and(jnp.logical_and(i >= 0, i < per * last), to > z))
        def _():
            act(to, lax.rem(i, per), True)

        j = t - (last - z)
        to_down = j // per

        @pl.when(jnp.logical_and(jnp.logical_and(j >= 0, j < per * last), to_down < z))
        def _():
            act(to_down, lax.rem(j, per), False)

    def x_stage(to, v, up):
        @pl.when(v >= 2)
        def _():
            x_send(to, v - 2)

    def slot(t, carry):
        stage(t, x_stage)

        own = t - per * last

        @pl.when(jnp.logical_and(own >= 0, own < UNITS - 1))
        def _():
            x_send(z, own)

        stage(t - lead, z_send)
        return carry

    lax.fori_loop(0, per * last + max(lead + last, UNITS - 1), slot, 0)

    def arrived(v, total):
        def plus(up, down):
            value = total
            if up:
                z_copy(z, v, True).wait_recv()
                value = value + wide(ur[z, pl.ds(v * n, n)])
            if down:
                z_copy(z, v, False).wait_recv()
                value = value + wide(dr[z, pl.ds(v * n, n)])
            return value

        return plus

    def finish(v, total, store):
        plus = arrived(v, total)

        @pl.when(z == 0)
        def _():
            store(plus(False, True))

        @pl.when(z == last)
        def _():
            store(plus(True, False))

        @pl.when(jnp.logical_and(z > 0, z < last))
        def _():
            store(plus(True, True))

    def keep(value):
        gv[z, 1 - x, piece(UNITS - 1)] = value.astype(gv.dtype)

    finish(0, both_cores(z, 1 - x, UNITS - 1), keep)
    x_copy(z, UNITS - 1).start()
    for v in tuple(range(2, per)) + (1,):
        u = UNITS - 1 if v == 1 else v - 2
        total = both_cores(z, x, u)
        x_copy(z, u).wait_recv()
        total = total + wide(xr[z, piece(u)])

        def put(value, u=u):
            out[piece(u)] = value

        finish(v, total, put)

    def sent(zo, carry):
        for v in range(per):
            @pl.when(zo > z)
            def _():
                z_copy(zo, v, True).wait_send()

            @pl.when(zo < z)
            def _():
                z_copy(zo, v, False).wait_send()
        for u in range(UNITS - 1):
            x_copy(zo, u).wait_send()

        @pl.when(zo == z)
        def _():
            x_copy(zo, UNITS - 1).wait_send()

        for xb in range(2):
            for u in range(UNITS):
                c_copy(zo, xb, u).wait_send()
        return carry

    lax.fori_loop(0, line, sent, 0)


def scatter(g, line, cid, name, lead=2):
    block = g.shape[3:]
    rows = block[0]
    n = rows // UNITS
    dma = pltpu.SemaphoreType.DMA
    per = UNITS + 1
    items = line * per
    vm = lambda *shape: pltpu.VMEM(shape + block[1:], g.dtype)
    return pl.pallas_call(
        functools.partial(scatter_kernel, line, lead),
        out_shape=jax.ShapeDtypeStruct(block, jnp.float32),
        in_specs=[pl.BlockSpec(memory_space=pl.ANY)],
        out_specs=pl.BlockSpec(memory_space=pltpu.VMEM),
        scratch_shapes=[vm(line, 2, rows), vm(line, 2, rows), vm(line, rows), vm(line, per * n), vm(line, per * n),
                        dma((line * 2 * UNITS,)), dma((line * 2 * UNITS,)), dma((line * 2 * UNITS,)),
                        dma((line * UNITS,)), dma((line * UNITS,)), dma((items,)), dma((items,)), dma((items,)), dma((items,))],
        compiler_params=pltpu.CompilerParams(collective_id=cid, has_side_effects=True, vmem_limit_bytes=50 * 2**20),
        name=name,
    )(g)


F32, BF16 = jnp.float32, jnp.bfloat16
NT = (((1,), (1,)), ((), ()))
TN = (((0,), (0,)), ((), ()))
norm_eps = 1e-12
masked_score = -1000000000.0
other_sequence = -3.0e38


def dot(a, b, dims=(((1,), (0,)), ((), ()))):
    return lax.dot_general(a, b, dims, preferred_element_type=F32)


class Block:
    def __init__(self, width, other, inner, hidden, heads, length, other_length, seqs, base=0):
        self.width, self.other, self.inner, self.hidden, self.heads = width, other, inner, hidden, heads
        self.length, self.other_length, self.seqs = length, other_length, seqs
        self.rows, self.other_rows = length * seqs, other_length * seqs
        self.base = base
        self.place = {}
        self.parts = []
        tile, flat = 0, 0

        def matrix(name, k, n):
            nonlocal tile, flat
            self.place[name] = (tile, k, n)
            self.parts.append((tile, flat, k, k * n // 128, n // 128))
            tile, flat = tile + k * n // 2048, flat + k * n // 128

        def vectors(*names):
            nonlocal tile, flat
            rows = 0
            for name, size in names:
                self.place[name] = (tile, rows, size)
                rows += size // 128
            self.parts.append((tile, flat, 0, rows, 0))
            tile, flat = tile + (rows + 15) // 16, flat + rows

        matrix("q_w", width, inner)
        vectors(("q_b", inner))
        matrix("k_w", other, inner)
        matrix("v_w", other, inner)
        vectors(("v_b", inner))
        matrix("o_w", inner, width)
        vectors(("o_b", width), ("g1", width), ("b1", width))
        matrix("i_w", width, hidden)
        vectors(("i_b", hidden))
        matrix("f_w", hidden, width)
        vectors(("f_b", width), ("g2", width), ("b2", width))
        self.tiles, self.flat_rows = tile, flat


VECS = ("q_b", "v_b", "o_b", "g1", "b1", "i_b", "f_b", "g2", "b2")
GROUPS = (("q_b",), ("v_b",), ("o_b", "g1", "b1"), ("i_b",), ("f_b", "g2", "b2"))


def cols(j, size=256):
    return pl.ds(pl.multiple_of(j * size, size), size)


class Net:
    def __init__(self, b, w, vec, sc):
        self.b, self.w, self.vec, self.s = b, w, vec, sc

    def mat(self, name):
        tile, k, n = self.b.place[name]
        return self.w.at[pl.ds(self.b.base + tile, k * n // 2048)].reshape(k // 16, n // 128, 16, 128)

    def row(self, name, j=None):
        k = VECS.index(name)
        size = self.b.place[name][2]
        return self.vec[k : k + 1, :size] if j is None else self.vec[k : k + 1, cols(j)]

    def load_vectors(self):
        for group in GROUPS:
            tile = self.b.place[group[0]][0]
            rows = sum(self.b.place[g][2] for g in group) // 128
            count = (rows + 15) // 16
            value = self.w[pl.ds(self.b.base + tile, count)].reshape(count * 16, 128).astype(F32)
            r = 0
            for name in group:
                k = VECS.index(name)
                for j in range(self.b.place[name][2] // 128):
                    self.vec[k : k + 1, j * 128 : (j + 1) * 128] = value[r : r + 1]
                    r += 1

    def store_vectors(self, group, scratch):
        tile = self.b.place[group[0]][0]
        rows = sum(self.b.place[g][2] for g in group) // 128
        count = (rows + 15) // 16
        scratch[0 : count * 16] = jnp.zeros((count * 16, 128), F32)
        r = 0
        for name in group:
            k = VECS.index(name)
            for j in range(self.b.place[name][2] // 128):
                scratch[r : r + 1, :] = self.vec[k : k + 1, j * 128 : (j + 1) * 128]
                r += 1
        self.w[pl.ds(self.b.base + tile, count)] = scratch[0 : count * 16].astype(BF16).reshape(count, 16, 128)

    def nn(self, x, name, put, step=256):
        m = self.mat(name)
        k, n = self.b.place[name][1:]

        def body(j, carry):
            per = step // 128
            w = jnp.concatenate([m[:, per * j + i].reshape(k, 128) for i in range(per)], axis=1)
            put(j, dot(x[...], w))
            return carry

        lax.fori_loop(0, n // step, body, 0)

    def nt(self, g, name, put, step=256):
        m = self.mat(name)
        k, n = self.b.place[name][1:]

        def body(j, carry):
            strips = step // 16
            w = jnp.concatenate(
                [m[pl.ds(j * strips, strips), i].reshape(step, 128) for i in range(n // 128)], axis=1)
            put(j, dot(g[...], w, NT))
            return carry

        lax.fori_loop(0, k // step, body, 0)

    def tn(self, a, g, name, step=256):
        m = self.mat(name)
        k, n = self.b.place[name][1:]
        per = step // 128

        def body(j, carry):
            got = dot(a[...], g[:, cols(j, step)], TN).astype(BF16)
            for i in range(per):
                m[:, per * j + i] = got[:, i * 128 : (i + 1) * 128].reshape(k // 16, 16, 128)
            return carry

        lax.fori_loop(0, n // step, body, 0)

    def norm(self, r, gain, shift):
        centre = r - jnp.mean(r, axis=-1, keepdims=True)
        spread = jnp.mean(centre * centre, axis=-1, keepdims=True)
        return centre * lax.rsqrt(spread + norm_eps) * self.row(gain) + self.row(shift)

    def norm_back(self, r, dy, gain, shift):
        centre = r - jnp.mean(r, axis=-1, keepdims=True)
        spread = jnp.mean(centre * centre, axis=-1, keepdims=True)
        s = lax.rsqrt(spread + norm_eps)
        xh = centre * s
        t = dy * self.row(gain)
        dr = s * (t - jnp.mean(t, axis=-1, keepdims=True) - xh * jnp.mean(t * xh, axis=-1, keepdims=True))
        size = self.b.width
        kg, kb = VECS.index(gain), VECS.index(shift)
        self.vec[kg : kg + 1, :size] = jnp.sum(dy * xh, axis=0, keepdims=True)
        self.vec[kb : kb + 1, :size] = jnp.sum(dy, axis=0, keepdims=True)
        return dr

    def put_sum(self, name, ref):
        k = VECS.index(name)
        self.vec[k : k + 1, : self.b.place[name][2]] = jnp.sum(ref[...].astype(F32), axis=0, keepdims=True)

    def mask(self, fill, counts):
        b = self.b
        shape = (b.rows, b.other_rows)
        row = lax.broadcasted_iota(jnp.int32, shape, 0)
        col = lax.broadcasted_iota(jnp.int32, shape, 1)
        value = jnp.full(shape, other_sequence, F32)
        for q in range(b.seqs):
            mine = (row >= q * b.length) & (row < (q + 1) * b.length)
            mine = mine & (col >= q * b.other_length) & (col < (q + 1) * b.other_length)
            value = jnp.where(mine, jnp.where(col < q * b.other_length + counts(q), 1.0, masked_score), value)
        fill[...] = value

    def heads_of(self, refs, g):
        e = self.b.inner // self.b.heads
        values = [ref[:, cols(g, 128)] for ref in refs]
        if e == 128:
            return [values]
        lane = lax.broadcasted_iota(jnp.int32, (1, 128), 1)
        return [
            [jnp.where((lane >= h * e) & (lane < (h + 1) * e), value, jnp.zeros((), BF16)) for value in values]
            for h in range(128 // e)]

    def attend(self, q, k, v, fill, p, c):
        b = self.b
        e = b.inner // b.heads
        scale = 1.0 / math.sqrt(e)
        per = max(128 // e, 1)

        def body(g, carry):
            keys = k[:, cols(g, 128)]
            total = None
            for h, (qh,) in enumerate(self.heads_of([q], g)):
                vh = self.heads_of([v], g)[h][0]
                s = dot(qh, keys, NT) * scale
                f = fill[...]
                s = jnp.where(f > 0, s, f)
                ex = jnp.exp(s - jnp.max(s, axis=-1, keepdims=True))
                probs = (ex * (1.0 / jnp.sum(ex, axis=-1, keepdims=True))).astype(BF16)
                p[g * per + h] = probs
                got = dot(probs, vh)
                total = got if total is None else total + got
            c[:, cols(g, 128)] = total.astype(BF16)
            return carry

        lax.fori_loop(0, b.inner // 128, body, 0)

    def attend_back(self, q, k, v, p, dc, dq, dk, dv):
        b = self.b
        e = b.inner // b.heads
        scale = 1.0 / math.sqrt(e)
        per = max(128 // e, 1)

        def body(g, carry):
            values = v[:, cols(g, 128)]
            sums = None
            for h, (qh, kh, dh) in enumerate(self.heads_of([q, k, dc], g)):
                probs = p[g * per + h]
                dp = dot(dh, values, NT)
                wide = probs.astype(F32)
                ds = (wide * (dp - jnp.sum(wide * dp, axis=-1, keepdims=True))).astype(BF16)
                got = [dot(ds, kh), dot(ds, qh, TN), dot(probs, dh, TN)]
                sums = got if sums is None else [x + y for x, y in zip(sums, got)]
            dq[:, cols(g, 128)] = (sums[0] * scale).astype(BF16)
            dk[:, cols(g, 128)] = (sums[1] * scale).astype(BF16)
            dv[:, cols(g, 128)] = sums[2].astype(BF16)
            return carry

        lax.fori_loop(0, b.inner // 128, body, 0)

    def forward(self, x, u, z, counts):
        s, b = self.s, self.b
        self.load_vectors()
        self.mask(s["fill"], counts)

        def put(ref, bias=None):
            def store(j, value):
                if bias is not None:
                    value = value + self.row(bias, j)
                ref[:, cols(j)] = value.astype(BF16)
            return store

        self.nn(u, "q_w", put(s["q"], "q_b"))
        self.nn(z, "k_w", put(s["k"]))
        self.nn(z, "v_w", put(s["v"], "v_b"))
        self.attend(s["q"], s["k"], s["v"], s["fill"], s["p"], s["c"])

        def first(j, value):
            s["r1"][:, cols(j)] = x[:, cols(j)].astype(F32) + (value + self.row("o_b", j))

        self.nn(s["c"], "o_w", first)
        y1 = self.norm(s["r1"][...], "g1", "b1")
        s["r2"][...] = y1
        s["y1"][...] = y1.astype(BF16)

        def up(j, value):
            value = value + self.row("i_b", j)
            half = 0.5 * (1.0 + lax.erf(value * (1.0 / math.sqrt(2.0))))
            s["a"][:, cols(j)] = (value * half).astype(BF16)
            s["gp"][:, cols(j)] = (half + value * (jnp.exp(-0.5 * value * value) * (1.0 / math.sqrt(2.0 * math.pi)))).astype(BF16)

        self.nn(s["y1"], "i_w", up)

        def second(j, value):
            s["r2"][:, cols(j)] = s["r2"][:, cols(j)] + (value + self.row("f_b", j))

        self.nn(s["a"], "f_w", second)
        return self.norm(s["r2"][...], "g2", "b2")

    def backward(self, dy, u, z, put_resid, put_z, done):
        s, b = self.s, self.b
        small = s["small"]
        dr2 = self.norm_back(s["r2"][...], dy[...], "g2", "b2")
        dy[...] = dr2
        s["m"][...] = dr2.astype(BF16)
        self.put_sum("f_b", s["m"])

        def inner(j, value):
            s["dz"][:, cols(j)] = (value * s["gp"][:, cols(j)].astype(F32)).astype(BF16)

        self.nt(s["m"], "f_w", inner)
        self.store_vectors(GROUPS[4], small)
        self.tn(s["a"], s["m"], "f_w")
        done(("f_w", "f_b"))
        self.put_sum("i_b", s["dz"])

        def mid(j, value):
            dy[:, cols(j)] = dy[:, cols(j)] + value

        self.nt(s["dz"], "i_w", mid)
        self.store_vectors(GROUPS[3], small)
        self.tn(s["y1"], s["dz"], "i_w")
        done(("i_w", "i_b"))
        dr1 = self.norm_back(s["r1"][...], dy[...], "g1", "b1")
        dy[...] = dr1
        s["m"][...] = dr1.astype(BF16)
        self.put_sum("o_b", s["m"])

        def context(j, value):
            s["dc"][:, cols(j)] = value.astype(BF16)

        self.nt(s["m"], "o_w", context)
        self.store_vectors(GROUPS[2], small)
        self.tn(s["c"], s["m"], "o_w")
        done(("o_w", "o_b"))
        self.attend_back(s["q"], s["k"], s["v"], s["p"], s["dc"], s["dq"], s["dk"], s["dv"])

        def resid(j, value):
            put_resid(j, dy[:, cols(j)] + value)

        self.nt(s["dq"], "q_w", resid)
        m = self.mat("v_w")
        mk = self.mat("k_w")
        k, n = b.place["v_w"][1:]

        def body(j, carry):
            def rows_of(mm):
                return jnp.concatenate([mm[pl.ds(j * 16, 16), i].reshape(256, 128) for i in range(n // 128)], axis=1)
            put_z(j, dot(s["dk"][...], rows_of(mk), NT) + dot(s["dv"][...], rows_of(m), NT))
            return carry

        lax.fori_loop(0, k // 256, body, 0)
        self.put_sum("q_b", s["dq"])
        self.put_sum("v_b", s["dv"])
        self.store_vectors(GROUPS[0], small)
        self.store_vectors(GROUPS[1], small)
        self.tn(u, s["dq"], "q_w")
        self.tn(z, s["dk"], "k_w")
        self.tn(z, s["dv"], "v_w")
        done(("q_w", "q_b", "k_w", "v_w", "v_b"))


def scratch_of(b):
    return {
        "q": ((b.rows, b.inner), BF16), "k": ((b.other_rows, b.inner), BF16), "v": ((b.other_rows, b.inner), BF16),
        "p": ((b.heads, b.rows, b.other_rows), BF16), "c": ((b.rows, b.inner), BF16),
        "r1": ((b.rows, b.width), F32), "r2": ((b.rows, b.width), F32), "y1": ((b.rows, b.width), BF16),
        "a": ((b.rows, b.hidden), BF16), "gp": ((b.rows, b.hidden), BF16), "fill": ((b.rows, b.other_rows), F32)}


def scratch_back(bs):
    rows, width = bs[0].rows, bs[0].width
    inner = max(b.inner for b in bs)
    other = max(b.other_rows for b in bs)
    return {
        "m": ((rows, width), BF16), "dz": ((rows, bs[0].hidden), BF16)}


def compute_kernel(co, sa, lens, x, xp, gy, wco, wsa, out, own_grad, sent, gco, gsa, wc, ws, vec, vec2, small, sems, *scr):
    names = sorted(scratch_of(co))
    sc = dict(zip(names, scr[: len(names)]))
    ss = dict(zip(names, scr[len(names) : 2 * len(names)]))
    rest = scr[2 * len(names) :]
    m, dz, dy, h, hb, dqc, dkc, dvc, dcc, dqs, dks, dvs, dcs = rest
    for d, extra in ((sc, (dqc, dkc, dvc, dcc)), (ss, (dqs, dks, dvs, dcs))):
        d["m"], d["dz"], d["small"] = m, dz, small
        d["dq"], d["dk"], d["dv"], d["dc"] = extra
    copies = [pltpu.make_async_copy(wco, wc, sems.at[0]), pltpu.make_async_copy(wsa, ws, sems.at[1])]
    for cp in copies:
        cp.start()
    copies[0].wait()
    a = Net(co, wc, vec, sc)
    bnet = Net(sa, ws, vec2, ss)
    value = a.forward(x, x, xp, lambda q: lens[1, q])
    h[...] = value
    hb[...] = value.astype(BF16)
    copies[1].wait()
    out[...] = bnet.forward(h, hb, hb, lambda q: lens[0, q]).astype(BF16)
    dy[...] = gy[...].astype(F32)

    def put_h(j, value):
        h[:, cols(j)] = value

    def add_h(j, value):
        h[:, cols(j)] = h[:, cols(j)] + value

    bnet.backward(dy, hb, hb, put_h, add_h, lambda names: None)
    back = pltpu.make_async_copy(ws, gsa, sems.at[1])
    back.start()

    def put_own(j, value):
        own_grad[:, cols(j)] = value

    def put_sent(j, value):
        sent[:, cols(j)] = value.astype(BF16)

    a.backward(h, x, xp, put_own, put_sent, lambda names: None)
    back2 = pltpu.make_async_copy(wc, gco, sems.at[0])
    back2.start()
    back.wait()
    back2.wait()


def compute(co, sa, lens, x, xp, gy, wco, wsa):
    any_ = pl.BlockSpec(memory_space=pl.ANY)
    vm = pl.BlockSpec(memory_space=pltpu.VMEM)
    names = sorted(scratch_of(co))
    V = lambda shape, dtype: pltpu.VMEM(shape, dtype)
    scr = [V(wco.shape, BF16), V(wsa.shape, BF16), V((16, 3072), F32), V((16, 3072), F32), V((32, 128), F32), pltpu.SemaphoreType.DMA((2,))]
    scr += [V(*scratch_of(co)[n]) for n in names] + [V(*scratch_of(sa)[n]) for n in names]
    rows, width = co.rows, co.width
    scr += [V((rows, width), BF16), V((rows, co.hidden), BF16), V((rows, width), F32), V((rows, width), F32), V((rows, width), BF16)]
    for b in (co, sa):
        scr += [V((b.rows, b.inner), BF16), V((b.other_rows, b.inner), BF16), V((b.other_rows, b.inner), BF16), V((b.rows, b.inner), BF16)]
    return pl.pallas_call(
        functools.partial(compute_kernel, co, sa),
        out_shape=(jax.ShapeDtypeStruct((rows, width), BF16), jax.ShapeDtypeStruct((rows, width), F32),
                   jax.ShapeDtypeStruct((co.other_rows, co.other), BF16),
                   jax.ShapeDtypeStruct(wco.shape, BF16), jax.ShapeDtypeStruct(wsa.shape, BF16)),
        in_specs=[pl.BlockSpec(memory_space=pltpu.SMEM), vm, vm, vm, any_, any_],
        out_specs=(vm, vm, vm, any_, any_),
        scratch_shapes=scr,
        compiler_params=pltpu.CompilerParams(vmem_limit_bytes=63 * 2**20),
        name="compute",
    )(lens, x, xp, gy, wco, wsa)


DT, HT, FT = 768, 12, 3072
DI, HI, FI = 1024, 8, 1024
DC, HC = 1024, 8
LT, LI = 128, 96
LINE_MAX = 8


def blocks_of(text, seqs):
    if text:
        return (Block(DT, DI, DC, FT, HC, LT, LI, seqs), Block(DT, DT, DT, FT, HT, LT, LT, seqs))
    return (Block(DI, DT, DC, FI, HC, LI, LT, seqs), Block(DI, DI, DI, FI, HI, LI, LI, seqs))


def flat_row(part, tile):
    first, flat, k, rows, nb = part
    t = tile - first
    return flat + (t // nb) * 16 * nb + t % nb if k else flat + t * 16


class Plan:
    def __init__(self, blocks, devices, flat_total):
        self.blocks = blocks
        self.shard = flat_total // 128 // devices
        tiles = max(b.tiles for b in blocks)
        self.rows = -(-tiles // (devices * UNITS)) * UNITS
        self.tiles = self.rows * devices
        before = after = 0
        for b in blocks:
            for d in range(devices):
                lo, hi = self.rows * d, self.rows * (d + 1)
                for part in b.parts:
                    first, flat, k, rows, nb = part
                    count = rows // 16 if k else (rows + 15) // 16
                    a, z = max(lo, first), min(hi, first + count)
                    if a >= z:
                        continue
                    least = min(flat_row(part, t) for t in range(a, min(z, a + max(nb, 1))))
                    reach = 15 * nb if k else 15
                    most = max(flat_row(part, t) for t in range(max(a, z - max(nb, 1)), z)) + reach
                    before = max(before, self.shard * d - least)
                    after = max(after, most + 1 - self.shard * (d + 1))
        self.before = -(-before // 16) * 16
        self.after = -(-after // 16) * 16
        self.window = -(-(self.before + self.shard + self.after) // 8) * 8

    def table(self, b):
        index = np.full((self.tiles * 16,), -1, np.int32)
        for first, flat, k, rows, nb in b.parts:
            if k:
                r, j = np.arange(k)[:, None], np.arange(nb)[None]
                at = first * 16 + ((r // 16) * nb + j) * 16 + r % 16
                index[at.reshape(-1)] = (flat + r * nb + j).reshape(-1)
            else:
                index[first * 16 : first * 16 + rows] = flat + np.arange(rows)
        return index


def each_tile(plan, b, d, act):
    lo = plan.rows * d
    start = plan.shard * d - plan.before
    for part in b.parts:
        first, flat, k, rows, nb = part
        if k:
            count = rows // 16
            a = jnp.clip(lo - first, 0, count)
            z = jnp.clip(lo + plan.rows - first, 0, count)

            def body(t, carry, first=first, flat=flat, nb=nb):
                i = t // nb
                act(first + t - lo, flat + i * 16 * nb + (t - i * nb) - start, nb, 16)
                return carry

            lax.fori_loop(a, z, body, 0)
        else:
            for t in range((rows + 15) // 16):
                here = jnp.logical_and(first + t >= lo, first + t < lo + plan.rows)

                @pl.when(here)
                def _(t=t, first=first, flat=flat, rows=rows):
                    act(first + t - lo, flat + 16 * t - start, 1, min(16, rows - 16 * t))


def to_tiles_kernel(plan, b, d_ref, window, out):
    out[...] = jnp.zeros(out.shape, out.dtype)

    def act(tile, row, stride, rows):
        value = window[pl.ds(row, rows, stride=stride), :]
        if rows < 16:
            value = jnp.concatenate([value, jnp.zeros((16 - rows, 128), value.dtype)], axis=0)
        out[tile] = value.astype(out.dtype)

    each_tile(plan, b, d_ref[0], act)


def from_tiles_kernel(plan, b, d_ref, tiles, window):
    window[...] = jnp.zeros(window.shape, window.dtype)

    def act(tile, row, stride, rows):
        window[pl.ds(row, rows, stride=stride), :] = tiles[tile][:rows]

    each_tile(plan, b, d_ref[0], act)


def by_stream(kernel, plan, text, d, value, shape, dtype, name):
    def call(b):
        def run(d, value):
            return pl.pallas_call(
                functools.partial(kernel, plan, b),
                out_shape=jax.ShapeDtypeStruct(shape, dtype),
                in_specs=[pl.BlockSpec(memory_space=pltpu.SMEM), pl.BlockSpec(memory_space=pltpu.VMEM)],
                out_specs=pl.BlockSpec(memory_space=pltpu.VMEM),
                compiler_params=pltpu.CompilerParams(vmem_limit_bytes=24 * 2**20),
                name=name,
            )(d, value)

        return run

    return lax.cond(text, call(plan.blocks[0]), call(plan.blocks[1]), d, value)


def shifted(value, axis, by):
    n = lax.axis_size(axis)
    return lax.ppermute(value, axis, [(i, i + by) for i in range(n) if 0 <= i + by < n])


def to_tiles(plan, text, d, flat):
    own = flat.reshape(plan.shard, 128)
    before = shifted(own[plan.shard - plan.before :], "dp", 1)
    after = shifted(own[: plan.after], "dp", -1)
    rest = jnp.zeros((plan.window - plan.before - plan.shard - plan.after, 128), own.dtype)
    window = jnp.concatenate([before, own, after, rest], axis=0)
    return by_stream(to_tiles_kernel, plan, text, d, window, (plan.rows, 16, 128), BF16, "to_tiles")


def from_tiles(plan, text, d, tiles):
    window = by_stream(from_tiles_kernel, plan, text, d, tiles, (plan.window, 128), F32, "from_tiles")
    end = plan.before + plan.shard
    own = window[plan.before : end]
    mine = shifted(window[end : end + plan.after], "dp", 1)
    own = own.at[: plan.after].add(mine)
    mine = shifted(window[: plan.before], "dp", -1)
    return own.at[plan.shard - plan.before :].add(mine).reshape(-1)


def gathered(plan, text, flat):
    whole = lax.all_gather(flat.astype(BF16), "dp", axis=0, tiled=True).reshape(-1, 128)
    index = jnp.where(text, *[jnp.asarray(plan.table(b)) for b in plan.blocks])
    rows = jnp.where((index >= 0)[:, None], whole[jnp.maximum(index, 0)], jnp.zeros((), BF16))
    return rows.reshape(plan.tiles, 16, 128)


def scattered(plan, text, tiles, flat_rows):
    tables = []
    for b in plan.blocks:
        table = plan.table(b)
        back = np.full((flat_rows,), -1, np.int32)
        held = np.nonzero(table >= 0)[0]
        back[table[held]] = held
        tables.append(jnp.asarray(back))
    index = jnp.where(text, *tables)
    rows = jnp.where((index >= 0)[:, None], tiles.reshape(-1, 128)[jnp.maximum(index, 0)], jnp.zeros((), BF16))
    return lax.psum_scatter(rows.astype(F32), "dp", scatter_dimension=0, tiled=True).reshape(-1)


def layer(text, counts, own, partner, grad, wco, wsa):
    seqs = own.shape[0]
    co, sa = blocks_of(text, seqs)
    box = own.shape
    lens = counts if text else counts[::-1]
    out, own_grad, sent, gco, gsa = compute(
        co, sa, lens, own.reshape(co.rows, co.width), partner.reshape(co.other_rows, co.other),
        grad.reshape(co.rows, co.width), wco, wsa)
    return out.reshape(box), own_grad.reshape(box), sent.reshape(box), gco, gsa


def body(devices, states, out_grad, co_params, self_params, text_lengths, region_counts):
    own = states[0]
    seqs = own.shape[0]
    text = lax.axis_index("stream") == 0
    d = lax.axis_index("dp").astype(jnp.int32).reshape(1)
    kinds = [[blocks_of(t, seqs)[i] for t in (True, False)] for i in range(2)]
    flats = (co_params[0], self_params[0])
    plans = [Plan(k, devices, f.shape[0] * devices) for k, f in zip(kinds, flats)]
    line = devices // 4
    near = devices % 4 == 0 and line <= LINE_MAX and all(p.before <= p.shard and p.after <= p.shard for p in plans)
    swap = [(0, 1), (1, 0)]
    partner = lax.ppermute(own, "stream", swap)
    if near:
        tiles = [to_tiles(p, text, d, f) for p, f in zip(plans, flats)]
        wco = gather(tiles[0], line, 1, "gather_co").reshape(plans[0].tiles, 16, 128)
        wsa = gather(tiles[1], line, 2, "gather_self").reshape(plans[1].tiles, 16, 128)
    else:
        wco, wsa = [gathered(p, text, f) for p, f in zip(plans, flats)]
    counts = jnp.stack([text_lengths, region_counts])
    out, own_grad, sent, gco, gsa = lax.cond(
        text, functools.partial(layer, True), functools.partial(layer, False),
        counts, own, partner, out_grad[0], wco, wsa)
    returned = lax.ppermute(sent, "stream", swap)
    grads = []
    for plan, g, cid, name in ((plans[1], gsa, 3, "scatter_self"), (plans[0], gco, 4, "scatter_co")):
        if near:
            block = scatter(g.reshape(line, 2, 2, plan.rows, 16, 128), line, cid, name)
            grads.append(from_tiles(plan, text, d, block))
        else:
            grads.append(scattered(plan, text, g, plan.shard * devices))
    states_grad = own_grad + returned.astype(F32)
    return (out[None], states_grad[None], grads[1][None], grads[0][None])


def solution(mesh):
    states = P("stream", "dp", None, None)
    flat = P("stream", "dp")
    return jax.shard_map(
        functools.partial(body, mesh.shape["dp"]), mesh=mesh, in_specs=(states, states, flat, flat, P("dp"), P("dp")),
        out_specs=(states, states, flat, flat), check_vma=False)
```

time: 2470 us -> 598 us (0.24); the launches traced: 2430 us -> 588 us
  local copies, waits for them, and re-layouts: 757 us -> 49.1 us
  blocking collectives: 653 us -> 0 us
  other arithmetic: 690 us -> 43.9 us
  Pallas kernels: 0 us -> 455 us
  matrix products: 136 us -> 0 us
  waiting for transfers between devices: 140 us -> 5.94 us
    all_gather x2 -> x0, other arithmetic: 657 us -> none  [the longest x1 356 us: body(): lax.all_gather(co_params[0].astype(jnp.bfloat16), 'dp', axis=0, tiled=True)]
    unnamed x2 -> x0, blocking collectives: 653 us -> none
    pallas_call x0 -> x9, Pallas kernels: none -> 455 us  [the longest x2 183 us: scatter(): pl.pallas_call(functools.partial(scatter_kernel, line, lead), out_shape=j...]
    cond x262 -> x0, local copies, waits for them, and re-layouts: 450 us -> none
    all_gather x2 -> x0, waiting for transfers between devices: 140 us -> none  [the longest x1 140 us: body(): lax.all_gather(self_params[0].astype(jnp.bfloat16), 'dp', axis=0, tiled=T...]
    dot_general x55 -> x0, matrix products: 136 us -> none  [the longest x17 66.4 us: product(): return jnp.dot(left_side, right_side, preferred_element_type=jnp.float32)]
    reshape x28 -> x1, local copies, waits for them, and re-layouts: 111 us -> 1.32 us  [layer(): own_grad.reshape(box)]
    slice x14 -> x8, local copies, waits for them, and re-layouts: 66.3 us -> 6.91 us  [the longest x2 2.94 us: to_tiles(): after = shifted(own[:plan.after], 'dp', -1)]
  transfers between devices with their start and end apart: 6 -> 8, of which waited for: 1 -> 1; matrix products, arithmetic and copies ran while one was open for 59% -> 12% of each run, Pallas kernels for 0% -> 44%
where the time goes in v1:
time: 598 us; the launch traced here: 588 us
  Pallas kernels  455 us (76%)
  local copies, waits for them, and re-layouts  49.1 us (8%)
  other arithmetic  43.9 us (7%)
  starting transfers between devices  23.1 us (4%)
  loops' own time  9.35 us (2%)
    pallas_call x2, Pallas kernels, scatter(): pl.pallas_call(functools.partial(scatter_kernel, line, lead), out_shape=j...  183 us
    pallas_call x2, Pallas kernels, gather(): pl.pallas_call(functools.partial(gather_kernel, line), out_shape=jax.Shap...  163 us
    pallas_call x1, Pallas kernels, compute(): pl.pallas_call(functools.partial(compute_kernel, co, sa), out_shape=(jax....  92.8 us
    unnamed x2, other arithmetic  39.7 us
    ppermute x6, starting transfers between devices, shifted(): lax.ppermute(value, axis, [(i, i + by) for i in range(n) if 0 <= i + by <...  21.7 us
    unnamed x16, local copies, waits for them, and re-layouts  21.3 us
    pallas_call x4, Pallas kernels, run(): pl.pallas_call(functools.partial(kernel, plan, b), out_shape=jax.ShapeDty...  16.4 us
  transfers between devices with their start and end apart: 8, of which 1 were waited for; matrix products, arithmetic and copies ran while one was open for 12% of the time, Pallas kernels for 44%

profile of v1, /device:TPU:9, one launch (start us, length us, event | category | flops | bytes accessed | tf_op | source)
XLA Modules:
  0.0 587.6 jit_solution(2267499124108504986)
XLA Ops:
  0.6 2.0 slice.96
  2.6 2.6 collective-permute-start.3
  5.2 1.3 collective-permute-start
  6.5 1.0 slice.94
  7.5 3.0 collective-permute-start.2
  10.5 0.8 slice.92
  11.3 2.5 collective-permute-start.1
  13.9 17.8 %reduce.7 = f32[443008]{0:T(1024)} reduce(f32[1,443008]{1,0:T(1,128)S(1)} %copy-done.4, f32[]{:T(128)} %constant.98), dimensions={0}, to_apply=%param.25.reduce_sub_computation | reduce | bytes 3544068 | tf_op args[3]
  31.7 22.0 %reduce.6 = f32[524928]{0:T(1024)} reduce(f32[1,524928]{1,0:T(1,128)} %param.24, f32[]{:T(128)} %constant.98), dimensions={0}, to_apply=%param.24.reduce_sub_computation | reduce | bytes 4199428 | tf_op args[2]
  53.6 0.0 collective-permute-done.1
  53.7 0.0 collective-permute-done.2
  53.7 5.6 concatenate.12
  59.3 4.2 conditional.5
  59.3 4.2 to_tiles.5
  63.5 87.4 %gather_co.1 = bf16[4,2,2,258,16,128]{5,4,3,2,1,0:T(8,128)(2,1)} custom-call(bf16[258,16,128]{2,1,0:T(8,128)(2,1)S(1)} %get-tuple-element.167.own), custom_call_target="tpu_custom_call" | custom-call | tf_op jit(solution)/shard_map/gather_co/pallas_call | solution.py:205
  150.8 0.0 collective-permute-done.3
  150.8 6.3 %concatenate.13 = f32[4792,128]{1,0:T(8,128)S(1)} concatenate(f32[3461,128]{1,0:T(8,128)} %bitcast.43, f32[1328,128]{1,0:T(8,128)} %collective-permute-done.3, f32[3,128]{1,0:T(4,128)S(1)} %broadcast.40), dimensions={0} | concatenate | bytes 4907008 | tf_op jit(solution)/shard_map/concatenate | solution.py:980
  157.2 4.2 conditional.6
  157.2 4.2 to_tiles.7
  161.4 75.5 %gather_self.1 = bf16[4,2,2,222,16,128]{5,4,3,2,1,0:T(8,128)(2,1)} custom-call(bf16[222,16,128]{2,1,0:T(8,128)(2,1)S(1)} %get-tuple-element.168.own), custom_call_target="tpu_custom_call" | custom-call | tf_op jit(solution)/shard_map/gather_self/pallas_call | solution.py:205
  236.9 109.6 %conditional.7 = (f32[2,96,1024]{2,1,0:T(8,128)S(1)}, bf16[2,96,1024]{2,1,0:T(8,128)(2,1)}, bf16[4128,16,128]{2,1,0:T(8,128)(2,1)}, bf16[3552,16,128]{2,1,0:T(8,128)(2,1)}, bf16[1,2,96,1024]{3,2,1,0:T(8,128)(2,1)}) conditional(s32[]{:T(128)} %convert_element_type.4, (s32[2,2]{1,0:T(2,128)S(1)}, bf16[1,2,96,1024]{3,2,1,0:T(8,128)(2,1)}, ...), branch_computations={%region_4.0_spmd, %region_5.0_spmd} | conditional | bytes 3932200 | solution.py:1044
  245.9 2.1 reshape_squeeze.14.x
  248.0 2.1 reshape_squeeze.15.gy
  250.0 92.8 %compute.3 = (bf16[256,768]{1,0:T(8,128)(2,1)}, f32[256,768]{1,0:T(8,128)}, bf16[192,1024]{1,0:T(8,128)(2,1)}, bf16[4128,16,128]{2,1,0:T(8,128)(2,1)}, bf16[3552,16,128]{2,1,0:T(8,128)(2,1)}) custom-call(s32[2,2]{1,0:T(2,128)S(1)} %get-tuple-element.124.lens, bf16[256,768]{1,0:T(8,128)(2,1)} %reshape_squeeze.14.x, bf16[192,1024]{1,0:T(8,128)(2,1)} %bitcast.4.xp, ...), custom_call_target="tpu_custom_call" | custom-call | tf_op jit(solution)/shard_map/cond/branch_1_fun/compute/pallas_call | solution.py:837
  342.8 1.3 reshape.113
  344.2 2.1 broadcast_in_dim.8
  346.5 99.0 %scatter_co.1 = f32[258,16,128]{2,1,0:T(8,128)S(1)} custom-call(bf16[4,2,2,258,16,128]{5,4,3,2,1,0:T(8,128)(2,1)} %bitcast.39), custom_call_target="tpu_custom_call" | custom-call | tf_op jit(solution)/shard_map/scatter_co/pallas_call | solution.py:423
  445.5 4.1 conditional.8
  445.5 4.1 from_tiles.5
  449.6 0.8 slice.108
  450.4 4.9 collective-permute-start.5
  455.3 83.8 %scatter_self.1 = f32[222,16,128]{2,1,0:T(8,128)S(1)} custom-call(bf16[4,2,2,222,16,128]{5,4,3,2,1,0:T(8,128)(2,1)} %bitcast.40), custom_call_target="tpu_custom_call" | custom-call | tf_op jit(solution)/shard_map/scatter_self/pallas_call | solution.py:423
  539.1 4.0 conditional.9
  539.1 3.9 from_tiles.7
  543.1 0.9 slice.113
  544.0 1.3 slice.111
  545.3 1.0 copy-done.1
  546.3 0.1 slice.106
  546.5 0.1 collective-permute-start.4
  546.5 6.5 %collective-permute-start.7 = (f32[1328,128]{1,0:T(8,128)}, f32[1328,128]{1,0:T(8,128)}, u32[]{:S(2)}, u32[]{:S(2)}) collective-permute-start(f32[1328,128]{1,0:T(8,128)} %slice.113), channel_id=1, source_target_pairs={{0,1},{1,2},{2,3},{3,4},{4,5},{5,6},{6,7},{7,8},{8,9},{9,10},{10,1... | collective-permute-start | bytes 2039816 | tf_op jit(solution)/shard_map/ppermute | solution.py:972
  553.0 2.2 collective-permute-start.6
  555.3 1.0 fusion.1
  556.3 5.9 %collective-permute-done.6 = f32[128,128]{1,0:T(8,128)S(1)} collective-permute-done((f32[128,128]{1,0:T(8,128)S(1)}, f32[128,128]{1,0:T(8,128)S(1)}, u32[]{:S(2)}, u32[]{:S(2)}) %collective-permute-start.6) | collective-permute-done | bytes 65568 | tf_op jit(solution)/shard_map/ppermute | solution.py:972
  562.2 1.5 scatter-add.11
  563.7 8.5 %copy.14 = f32[1,1,4101,128]{3,1,2,0:T(1,128)} copy(f32[1,1,4101,128]{3,2,1,0:T(8,128)} %bitcast.41) | data formatting | bytes 4199424
  572.2 2.0 add_bitcast_fusion
  574.2 1.2 fusion
  575.4 11.8 %copy.15 = f32[1,1,3461,128]{3,1,2,0:T(1,128)} copy(f32[1,1,3461,128]{3,2,1,0:T(8,128)S(1)} %bitcast.44) | data formatting | bytes 3544064
  (21 shorter events, 0.1 us)
Async XLA Ops:
  0.6 13.3 %copy-start.4 = (f32[1,443008]{1,0:T(1,128)S(1)}, f32[1,443008]{1,0:T(1,128)}, u32[]{:S(2)}) copy-start(f32[1,443008]{1,0:T(1,128)} %param.25) | copy-start | bytes 5316100
  2.6 148.2 %collective-permute-start.3 = (f32[1328,128]{1,0:T(8,128)}, f32[1328,128]{1,0:T(8,128)}, u32[]{:S(2)}, u32[]{:S(2)}) collective-permute-start(f32[1328,128]{1,0:T(8,128)} %bitcast.13), channel_id=1, source_target_pairs={{1,0},{2,1},{3,2},{4,3},{5,4},{6,5},{7,6},{8,7},{9,8},{10,9},{11,1... | collective-permute-start | bytes 2039816 | tf_op jit(solution)/shard_map/ppermute | solution.py:972
  5.2 231.7 %collective-permute-start = (bf16[2,96,1024]{2,1,0:T(8,128)(2,1)}, bf16[2,96,1024]{2,1,0:T(8,128)(2,1)}, u32[]{:S(2)}, u32[]{:S(2)}) collective-permute-start(bf16[2,96,1024]{2,1,0:T(8,128)(2,1)} %bitcast.8), channel_id=1, source_target_pairs={{0,16},{16,0},{1,17},{17,1},{2,18},{18,2},{3,19},{19,3},{4,20},{20... | collective-permute-start | bytes 1179656 | tf_op jit(solution)/shard_map/ppermute | solution.py:1036
  7.5 46.2 %collective-permute-start.2 = (f32[496,128]{1,0:T(8,128)S(1)}, f32[496,128]{1,0:T(8,128)S(1)}, u32[]{:S(2)}, u32[]{:S(2)}) collective-permute-start(f32[496,128]{1,0:T(8,128)S(1)} %bitcast.48), channel_id=1, source_target_pairs={{1,0},{2,1},{3,2},{4,3},{5,4},{6,5},{7,6},{8,7},{9,8},{10,9},{11,1... | collective-permute-start | bytes 761864 | tf_op jit(solution)/shard_map/ppermute | solution.py:972
  11.3 42.3 %collective-permute-start.1 = (f32[128,128]{1,0:T(8,128)S(1)}, f32[128,128]{1,0:T(8,128)S(1)}, u32[]{:S(2)}, u32[]{:S(2)}) collective-permute-start(f32[128,128]{1,0:T(8,128)S(1)} %bitcast.49), channel_id=1, source_target_pairs={{0,1},{1,2},{2,3},{3,4},{4,5},{5,6},{6,7},{7,8},{8,9},{9,10},{10,1... | collective-permute-start | bytes 196616 | tf_op jit(solution)/shard_map/ppermute | solution.py:972
  31.7 22.0 %copy-start.5 = (s32[2]{0:T(128)S(1)}, s32[2]{0:T(128)}, u32[]{:S(2)}) copy-start(s32[2]{0:T(128)} %param.27) | copy-start | bytes 28
  31.7 22.0 %copy-start.6 = (s32[2]{0:T(128)S(1)}, s32[2]{0:T(128)}, u32[]{:S(2)}) copy-start(s32[2]{0:T(128)} %param.26) | copy-start | bytes 28
  449.6 89.5 %copy-start = (f32[4728,128]{1,0:T(8,128)}, f32[4728,128]{1,0:T(8,128)S(1)}, u32[]{:S(2)}) copy-start(f32[4728,128]{1,0:T(8,128)S(1)} %get-tuple-element.169) | copy-start | bytes 7262212
  450.4 104.9 %collective-permute-start.5 = (f32[496,128]{1,0:T(8,128)}, f32[496,128]{1,0:T(8,128)}, u32[]{:S(2)}, u32[]{:S(2)}) collective-permute-start(f32[496,128]{1,0:T(8,128)} %slice.108), channel_id=1, source_target_pairs={{0,1},{1,2},{2,3},{3,4},{4,5},{5,6},{6,7},{7,8},{8,9},{9,10},{10,1... | collective-permute-start | bytes 761864 | tf_op jit(solution)/shard_map/ppermute | solution.py:972
  544.0 2.3 copy-start.1
  546.5 25.7 %collective-permute-start.4 = (bf16[2,96,1024]{2,1,0:T(8,128)(2,1)}, bf16[2,96,1024]{2,1,0:T(8,128)(2,1)}, u32[]{:S(2)}, u32[]{:S(2)}) collective-permute-start(bf16[2,96,1024]{2,1,0:T(8,128)(2,1)} %get-tuple-element.154), channel_id=1, source_target_pairs={{0,16},{16,0},{1,17},{17,1},{2,18},{18,2},{3,19},{19,3},{4,20},{20... | collective-permute-start | bytes 1179656 | tf_op jit(solution)/shard_map/ppermute | solution.py:1047
  546.5 27.6 %collective-permute-start.7 = (f32[1328,128]{1,0:T(8,128)}, f32[1328,128]{1,0:T(8,128)}, u32[]{:S(2)}, u32[]{:S(2)}) collective-permute-start(f32[1328,128]{1,0:T(8,128)} %slice.113), channel_id=1, source_target_pairs={{0,1},{1,2},{2,3},{3,4},{4,5},{5,6},{6,7},{7,8},{8,9},{9,10},{10,1... | collective-permute-start | bytes 2039816 | tf_op jit(solution)/shard_map/ppermute | solution.py:972
  553.0 9.1 %collective-permute-start.6 = (f32[128,128]{1,0:T(8,128)S(1)}, f32[128,128]{1,0:T(8,128)S(1)}, u32[]{:S(2)}, u32[]{:S(2)}) collective-permute-start(f32[128,128]{1,0:T(8,128)S(1)} %slice.110), channel_id=1, source_target_pairs={{1,0},{2,1},{3,2},{4,3},{5,4},{6,5},{7,6},{8,7},{9,8},{10,9},{11,1... | collective-permute-start | bytes 196616 | tf_op jit(solution)/shard_map/ppermute | solution.py:972
  556.2 5.9 %copy-start.2 = (f32[4101,128]{1,0:T(8,128)}, f32[4101,128]{1,0:T(8,128)S(1)}, u32[]{:S(2)}) copy-start(f32[4101,128]{1,0:T(8,128)S(1)} %fusion.1) | copy-start | bytes 6299140
  563.7 10.5 %copy-start.3 = (f32[3461,128]{1,0:T(8,128)S(1)}, f32[3461,128]{1,0:T(8,128)}, u32[]{:S(2)}) copy-start(f32[3461,128]{1,0:T(8,128)} %slice.111) | copy-start | bytes 5316100
